TPU v7x, 32 devices: a whole 2x2x4 slice. The times are simulated.
32 devices in a mesh: gx: 4 (over y, core), gy: 8 (over z, x).
Axes of the slice: x: 2, y: 2, z: 4, core: 2. Of those that a mesh axis runs over, the one named last changes fastest.
Arguments:
- displacement: float32 [3, 96, 64, 128], P(None, 'gx', 'gy'), may hold values from -6 to 6
- velocity: float32 [3, 96, 64, 128], P(None, 'gx', 'gy'), may hold values from -6 to 6
- external_force: float32 [3, 96, 64, 128], P(None, 'gx', 'gy'), may hold values from -6 to 6
- node_mass: float32 [96, 64, 128], P('gx', 'gy'), may hold values from 0.5 to 2
- stiffness: float32 [96, 64, 128], P('gx', 'gy'), may hold values from 0.5 to 2
- cloak_list: int32 [4, 8, 48], P('gx'), may hold values from -1 to 191, as said below
- micro_state: float32 [4, 8, 128, 48, 128], P('gx', 'gy'), may hold values from -6 to 6
- localization: float32 [256, 6], replicated, may hold values from -3.6 to 3.6
- modes: float32 [256, 128], replicated, may hold values from -0.5 to 0.5
- point_weight: float32 [256], replicated, may hold values from 0.5 to 2
- point_modulus: float32 [256], replicated, may hold values from 1 to 10
- softening: float32 [256], replicated, may hold values from 0.2 to 2
Outputs:
- displacement_next: float32 [3, 96, 64, 128], P(None, 'gx', 'gy')
- velocity_next: float32 [3, 96, 64, 128], P(None, 'gx', 'gy')
- micro_state_next: float32 [4, 8, 128, 48, 128], P('gx', 'gy')
Inputs may be any that keep to these rules, and one draw needn't show every extreme that they name: cloak_list[p, t, :] holds distinct pencil indices x * 8 + y of tile (p, t) in ascending order followed by -1; in every gx index exactly one tile lists 48 pencils and every other tile lists between 20 and 24 pencils, 20 reached in every gx index; the tiles sharing a gx index list exactly 192 pencils together.
All inputs are finite; a program needn't handle non-finite values.
Results may differ from a plain program's by a relative error of at most 0.0003.
Values sent between devices are 32-bit elements; how exact they have to be, the bound alone decides.
No kernel may reach another device: no remote copies, remote signals or barrier semaphores. Data moves between devices by JAX's collectives and lax.ppermute only.
A program may use at most 64 MiB of HBM per device.

v0:
```python
import functools

import jax
import jax.numpy as jnp
from jax import lax
from jax.experimental import pallas as pl
from jax.experimental.pallas import tpu as pltpu
from jax.sharding import PartitionSpec as P

ITERS = 3
STEP = 0.25
HIGHEST = lax.Precision.HIGHEST
F32 = jnp.float32
BF16 = jnp.bfloat16
VMEM = pl.BlockSpec(memory_space=pltpu.VMEM)
SMEM = pl.BlockSpec(memory_space=pltpu.SMEM)


def split(x):
    high = x.astype(BF16)
    return high, (x - high.astype(F32)).astype(BF16)


def dot(a, b):
    return jnp.dot(a, b, preferred_element_type=F32)


def exact(a, b):
    return jnp.dot(a, b, precision=HIGHEST, preferred_element_type=F32)


def inverse_rows(matrix):
    size = matrix.shape[0]
    blocks = [matrix[i : i + 8] for i in range(0, size, 8)]
    lane = lax.broadcasted_iota(jnp.int32, (8, size), 1)
    row = lax.broadcasted_iota(jnp.int32, (8, size), 0)
    for b in range(size // 8):
        panel = blocks[b]
        for s in range(8):
            k = b * 8 + s
            column = jnp.broadcast_to(panel[:, k : k + 1], (8, size))
            pivot_row = jnp.broadcast_to(panel[s : s + 1, :], (8, size))
            inverse = 1.0 / jnp.broadcast_to(column[s : s + 1, :], (8, size))
            new_row = jnp.where(lane == k, inverse, pivot_row * inverse)
            rest = jnp.where(lane == k, 0.0, panel) - column * new_row
            panel = jnp.where(row == s, new_row, rest)
        rows = [jnp.broadcast_to(panel[s : s + 1, :], (8, size)) for s in range(8)]
        inside = jnp.logical_and(lane >= b * 8, lane < b * 8 + 8)
        order = list(range(b + 1, size // 8)) + list(range(b))
        for i in order:
            old = blocks[i]
            new = jnp.where(inside, 0.0, old)
            for s in range(8):
                k = b * 8 + s
                new = new - jnp.broadcast_to(old[:, k : k + 1], (8, size)) * rows[s]
            blocks[i] = new
        blocks[b] = panel
    return jnp.concatenate(blocks, axis=0)


def matrices_kernel(
    modes_ref, local_ref, weight_ref, modulus_ref, soft_ref,
    first_ref, newton_ref, back_ref, stress_ref, wide,
):
    points, count = modes_ref.shape
    modes = modes_ref[...]
    modes_t = modes.T
    weight = weight_ref[...] / points
    modulus = modulus_ref[...]
    root = jnp.sqrt(soft_ref[...])
    matrix = exact(modes_t * (weight * modulus), modes)
    inverse = inverse_rows(matrix)
    scale = weight * modulus / root
    wide[...] = jnp.zeros_like(wide)
    wide[:, 0 : local_ref.shape[1]] = local_ref[...]
    local_t = wide[...].T
    stress_ref[...] = (local_t[0:16] * scale).astype(BF16)
    soft_modes = (modes_t * root).T
    soft_local = (local_t * root).T
    back = exact(inverse, modes_t * scale)
    newton = exact(soft_modes, back)
    high, low = split(soft_modes)
    first_ref[:, 0:count] = high
    first_ref[:, count : 2 * count] = high
    first_ref[:, 2 * count : 3 * count] = low
    shape = soft_local.shape
    lane = lax.broadcasted_iota(jnp.int32, shape, 1)
    moved8 = pltpu.roll(soft_local, 8, 1)
    moved16 = pltpu.roll(soft_local, 16, 1)
    high8 = (soft_local + moved8).astype(BF16).astype(F32)
    low16 = moved16 - moved16.astype(BF16).astype(F32)
    first_ref[:, 3 * count :] = jnp.where(lane < 16, high8, low16).astype(BF16)
    high, low = split(newton)
    newton_ref[:, 0:points] = high
    newton_ref[:, points : 2 * points] = low
    high, low = split(back)
    back_ref[:, 0:points] = high
    back_ref[:, points : 2 * points] = low


def respond(u):
    return u * lax.rsqrt(1.0 + u * u)


def cells(states, strains, first_ref, newton_ref, back_ref, stress_ref):
    points = newton_ref.shape[0]
    count = back_ref.shape[0]
    newton_high = newton_ref[:, 0:points]
    newton_low = newton_ref[:, points:]
    back_high = back_ref[:, 0:points]
    back_low = back_ref[:, points:]
    state_high, state_low = split(states)
    strain_high = strains.astype(BF16).astype(F32)
    strain_low = strains - strain_high
    zero = jnp.zeros_like(strains)
    strain_part = jnp.concatenate(
        [strain_high, strain_low, strain_high] + [zero] * (count // 8 - 3), axis=0
    ).astype(BF16)
    u = dot(first_ref[:, 0 : 2 * count], jnp.concatenate([state_high, state_low], axis=0))
    u = u + dot(first_ref[:, 2 * count :], jnp.concatenate([state_high, strain_part], axis=0))
    total = None
    for step in range(ITERS):
        h = respond(u)
        total = h if total is None else total + h
        if step < ITERS - 1:
            high, low = split(h)
            u = u - (dot(newton_high, high) + dot(newton_low, high) + dot(newton_high, low))
        else:
            u = u - dot(newton_high, h.astype(BF16))
    high, low = split(total)
    new_states = states - (dot(back_high, high) + dot(back_low, high) + dot(back_high, low))
    stress = dot(stress_ref[...], respond(u).astype(BF16))
    return new_states, stress[0:8]


def main_kernel(
    lists_ref, disp_ref, xhalo_ref, yhalo_ref, corner_ref, stiff_ref, state_ref,
    first_ref, newton_ref, back_ref, stress_ref,
    force_ref, xface_ref, yface_ref, cface_ref, out_ref,
    strain_s, stress_s,
):
    rows, columns, layers = stiff_ref.shape
    count = back_ref.shape[0]
    most = lists_ref.shape[1]
    tile = (columns, layers)
    lane = lax.broadcasted_iota(jnp.int32, tile, 1)
    sub = lax.broadcasted_iota(jnp.int32, tile, 0)
    last_lane = lane == layers - 1
    first_lane = lane == 0
    last_sub = sub == columns - 1
    first_sub = sub == 0
    member = lax.axis_index("gy")

    def node_row(c, i):
        own = disp_ref[c, i] if i < rows else xhalo_ref[c]
        edge = yhalo_ref[c, i : i + 1] if i < rows else corner_ref[c : c + 1]
        up = jnp.where(last_sub, jnp.broadcast_to(edge, tile), pltpu.roll(own, columns - 1, 0))
        mean, diff = 0.5 * (up + own), up - own
        mean_up = jnp.where(last_lane, 0.0, pltpu.roll(mean, layers - 1, 1))
        diff_up = jnp.where(last_lane, 0.0, pltpu.roll(diff, layers - 1, 1))
        return 0.5 * (mean_up + mean), 0.5 * (diff_up + diff), mean_up - mean

    lower = [node_row(c, 0) for c in range(3)]
    zero_tile = jnp.zeros(tile, F32)
    for i in range(rows):
        upper = [node_row(c, i + 1) for c in range(3)]
        g = [
            (upper[c][0] - lower[c][0], 0.5 * (upper[c][1] + lower[c][1]), 0.5 * (upper[c][2] + lower[c][2]))
            for c in range(3)
        ]
        lower = upper
        strain = [g[0][0], g[1][1], g[2][2], g[1][2] + g[2][1], g[0][2] + g[2][0], g[0][1] + g[1][0]]
        stiffness = stiff_ref[i]
        volume = strain[0] + strain[1] + strain[2]
        for c in range(8):
            place = pl.ds(i * columns * 8 + c, columns, stride=8)
            if c >= 6:
                strain_s[place, :] = zero_tile
                continue
            strain_s[place, :] = strain[c]
            stress_s[place, :] = stiffness * (volume + 2.0 * strain[c] if c < 3 else strain[c])

    group = 4

    def body(q, carry):
        base = q * group
        busy = lists_ref[member, base] >= 0

        @pl.when(busy)
        def _():
            for pair in range(group // 2):
                entries = [lists_ref[member, base + 2 * pair + s] for s in range(2)]
                places = [pl.multiple_of(jnp.maximum(e, 0) * 8, 8) for e in entries]
                slots = [pl.ds(base + 2 * pair + s, count, stride=most) for s in range(2)]
                states = jnp.concatenate([state_ref[slot, :] for slot in slots], axis=1)
                strains = jnp.concatenate([strain_s[pl.ds(p, 8), :] for p in places], axis=1)
                new_states, stress = cells(states, strains, first_ref, newton_ref, back_ref, stress_ref)
                for s in range(2):
                    part = new_states[:, s * layers : (s + 1) * layers]
                    out_ref[slots[s], :] = jnp.where(entries[s] >= 0, part, 0.0)

                    @pl.when(entries[s] >= 0)
                    def _():
                        stress_s[pl.ds(places[s], 8), :] = stress[:, s * layers : (s + 1) * layers]

        @pl.when(jnp.logical_not(busy))
        def _():
            for s in range(group):
                out_ref[pl.ds(base + s, count, stride=most), :] = jnp.zeros((count, layers), F32)

        return carry

    lax.fori_loop(0, most // group, body, 0)

    def fluxes(s, side_mean, side_diff, lane_zero):
        def along(v):
            down = jnp.where(lane_zero, 0.0, pltpu.roll(v, 1, 1))
            return 0.5 * (v + down), v - down

        first = [along(side_mean(s[c]))[0] for c in (0, 5, 4)]
        second = [along(side_diff(s[c]))[0] for c in (5, 1, 3)]
        third = [along(side_mean(s[c]))[1] for c in (4, 3, 2)]
        half = [0.5 * (second[c] + third[c]) for c in range(3)]
        return [(first[c] + half[c], half[c] - first[c]) for c in range(3)]

    def shift(v):
        return jnp.where(first_sub, 0.0, pltpu.roll(v, 1, 0))

    below = None
    for i in range(rows):
        s = [stress_s[pl.ds(i * columns * 8 + c, columns, stride=8), :] for c in range(6)]
        here = fluxes(s, lambda v: 0.5 * (v + shift(v)), lambda v: v - shift(v), first_lane)
        for c in range(3):
            force_ref[c, i] = -here[c][0] if below is None else -(here[c][0] + below[c][1])
        below = here
    for c in range(3):
        xface_ref[c] = -below[c][1]
    s = [stress_s[pl.ds((columns - 1) * 8 + c, rows, stride=columns * 8), :] for c in range(6)]
    wide_zero = lax.broadcasted_iota(jnp.int32, (rows, layers), 1) == 0
    side = fluxes(s, lambda v: 0.5 * v, lambda v: -v, wide_zero)
    for c in range(3):
        yface_ref[c] = -side[c][0]
        yface_ref[c, 1:rows] = yface_ref[c, 1:rows] - side[c][1][0 : rows - 1]
        cface_ref[c : c + 1] = -side[c][1][rows - 1 : rows]


def update_kernel(
    disp_ref, velocity_ref, external_ref, mass_ref, force_ref, xface_ref, yface_ref, cface_ref,
    disp_out, velocity_out,
):
    rows, columns, layers = mass_ref.shape
    first_sub = lax.broadcasted_iota(jnp.int32, (columns, layers), 0) == 0
    for i in range(rows):
        factor = STEP / mass_ref[i]
        for c in range(3):
            edge = yface_ref[c, i : i + 1]
            if i == 0:
                edge = edge + cface_ref[c : c + 1]
            internal = force_ref[c, i] + jnp.where(
                first_sub, jnp.broadcast_to(edge, (columns, layers)), 0.0
            )
            if i == 0:
                internal = internal + xface_ref[c]
            velocity = velocity_ref[c, i] + factor * (external_ref[c, i] - internal)
            velocity_out[c, i] = velocity
            disp_out[c, i] = disp_ref[c, i] + STEP * velocity


def shape(*dims, dtype=F32):
    return jax.ShapeDtypeStruct(dims, dtype)


def on_device(
    displacement, velocity, external_force, node_mass, stiffness, cloak_list, micro_state,
    localization, modes, point_weight, point_modulus, softening,
):
    rows, columns, layers = stiffness.shape
    points, count = modes.shape
    most = cloak_list.shape[2]
    gx, gy = lax.axis_size("gx"), lax.axis_size("gy")
    along_x = [(i + 1, i) for i in range(gx - 1)]
    along_y = [(i + 1, i) for i in range(gy - 1)]
    both = [((i + 1) * gy + j + 1, i * gy + j) for i in range(gx - 1) for j in range(gy - 1)]
    back = lambda pairs: [(b, a) for a, b in pairs]
    xhalo = lax.ppermute(displacement[:, 0], "gx", along_x)
    yhalo = lax.ppermute(displacement[:, :, 0], "gy", along_y)
    corner = lax.ppermute(displacement[:, 0, 0], ("gx", "gy"), both)

    first, newton, back_m, stress_m = pl.pallas_call(
        matrices_kernel,
        out_shape=(
            shape(points, 4 * count, dtype=BF16), shape(points, 2 * points, dtype=BF16),
            shape(count, 2 * points, dtype=BF16), shape(16, points, dtype=BF16),
        ),
        in_specs=[VMEM] * 5,
        out_specs=(VMEM,) * 4,
        scratch_shapes=[pltpu.VMEM((points, 128), F32)],
        compiler_params=pltpu.CompilerParams(vmem_limit_bytes=16 * 2**20),
        cost_estimate=pl.CostEstimate(flops=10**8, bytes_accessed=10**6, transcendentals=0),
    )(
        modes, localization, point_weight.reshape(1, points), point_modulus.reshape(1, points),
        softening.reshape(1, points),
    )

    force, xface, yface, cface, new_state = pl.pallas_call(
        main_kernel,
        out_shape=(
            shape(3, rows, columns, layers), shape(3, columns, layers), shape(3, rows, layers),
            shape(3, layers), shape(count * most, layers),
        ),
        in_specs=[SMEM] + [VMEM] * 10,
        out_specs=(VMEM,) * 5,
        scratch_shapes=[pltpu.VMEM((rows * columns * 8, layers), F32)] * 2,
        compiler_params=pltpu.CompilerParams(vmem_limit_bytes=40 * 2**20),
        cost_estimate=pl.CostEstimate(flops=10**10, bytes_accessed=10**7, transcendentals=0),
    )(
        cloak_list[0], displacement, xhalo, yhalo, corner, stiffness,
        micro_state.reshape(count * most, layers), first, newton, back_m, stress_m,
    )

    xface = lax.ppermute(xface, "gx", back(along_x))
    yface = lax.ppermute(yface, "gy", back(along_y))
    cface = lax.ppermute(cface, ("gx", "gy"), back(both))

    displacement_next, velocity_next = pl.pallas_call(
        update_kernel,
        out_shape=(shape(3, rows, columns, layers),) * 2,
        in_specs=[VMEM] * 8,
        out_specs=(VMEM,) * 2,
        compiler_params=pltpu.CompilerParams(vmem_limit_bytes=16 * 2**20),
    )(displacement, velocity, external_force, node_mass, force, xface, yface, cface)
    return displacement_next, velocity_next, new_state.reshape(micro_state.shape)


def solution(mesh):
    field = P(None, "gx", "gy", None)
    grid = P("gx", "gy", None)
    state = P("gx", "gy", None, None, None)
    in_specs = (field, field, field, grid, grid, P("gx", None, None), state, P(), P(), P(), P(), P())
    return jax.shard_map(
        on_device, mesh=mesh, in_specs=in_specs, out_specs=(field, field, state), check_vma=False
    )
```

profile of v0, /device:TPU:25, one launch (start us, length us, event | category | flops | bytes accessed | tf_op | source)
XLA Modules:
  0.0 82.9 jit_solution(9510203011307234187)
XLA Ops:
  0.6 1.0 %slice.10 = f32[3,24,1,128]{3,2,1,0:T(1,128)S(1)} slice(f32[3,24,8,128]{3,2,1,0:T(8,128)} %disp_ref.3), slice={[0:3], [0:24], [0:1], [0:128]} | slice | bytes 73728 | tf_op jit(solution)/shard_map/slice | solution.py:286
  1.6 3.0 %collective-permute-start.1 = (f32[3,24,128]{2,1,0:T(8,128)S(1)}, f32[3,24,128]{2,1,0:T(8,128)S(1)}, u32[]{:S(2)}, u32[]{:S(2)}) collective-permute-start(f32[3,24,128]{2,1,0:T(8,128)S(1)} %bitcast.21), channel_id=1, source_target_pairs={{1,0},{2,1},{3,2},{4,3},{5,4},{6,5},{7,6},{9,8},{10,9},{11,10},{12... | collective-permute-start | bytes 110600 | tf_op jit(solution)/shard_map/ppermute | solution.py:286
  4.6 0.7 slice_bitcast_fusion
  5.3 2.9 %collective-permute-start = (f32[3,8,128]{2,1,0:T(8,128)S(1)}, f32[3,8,128]{2,1,0:T(8,128)S(1)}, u32[]{:S(2)}, u32[]{:S(2)}) collective-permute-start(f32[3,8,128]{2,1,0:T(8,128)S(1)} %slice_bitcast_fusion), channel_id=1, source_target_pairs={{8,0},{16,8},{24,16},{9,1},{17,9},{25,17},{10,2},{18,10},{26,18},{... | collective-permute-start | bytes 36872 | tf_op jit(solution)/shard_map/ppermute | solution.py:285
  8.2 0.7 slice.11
  8.9 1.9 %collective-permute-start.2 = (f32[3,128]{1,0:T(4,128)S(1)}, f32[3,128]{1,0:T(4,128)S(1)}, u32[]{:S(2)}, u32[]{:S(2)}) collective-permute-start(f32[3,128]{1,0:T(4,128)S(1)} %bitcast.22), channel_id=1, source_target_pairs={{9,0},{10,1},{11,2},{12,3},{13,4},{14,5},{15,6},{17,8},{18,9},{19,... | collective-permute-start | bytes 4616 | tf_op jit(solution)/shard_map/ppermute | solution.py:287
  10.8 0.8 copy.18.local_ref
  11.7 0.0 copy-start.5
  11.7 0.9 %copy-done.5 = f32[256,128]{1,0:T(8,128)S(1)} copy-done((f32[256,128]{1,0:T(8,128)S(1)}, f32[256,128]{1,0:T(8,128)}, u32[]{:S(2)}) %copy-start.5) | copy-done | bytes 131096
  12.6 0.0 copy-start.8
  12.6 0.7 copy-done.8
  13.3 0.0 copy-start.9
  13.3 0.7 copy-done.9
  13.9 0.0 copy-start.10
  13.9 0.7 copy-done.10
  14.6 17.4 %shard_map.139 = (bf16[256,512]{1,0:T(8,128)(2,1)S(1)}, bf16[256,512]{1,0:T(8,128)(2,1)S(1)}, bf16[128,512]{1,0:T(8,128)(2,1)S(1)}, bf16[16,256]{1,0:T(8,128)(2,1)S(1)}) custom-call(f32[256,128]{1,0:T(8,128)S(1)} %copy-done.5, f32[256,6]{1,0:T(8,128)S(1)} %copy.18.local_ref, f32[1,256]{1,0:T(1,128)S(1)} %bitcast.18, f32[1,256]{1,0:T(1,128)S(1)} %bitcast.19, ...), custom_call_target="tpu_custom_call" | custom-call | flops 100000000 | bytes 1000000 | tf_op jit(solution)/shard_map/pallas_call | solution.py:289
  32.1 0.0 collective-permute-done.2.corner_ref
  32.1 0.0 collective-permute-done.xhalo_ref
  32.1 0.0 collective-permute-done.1.yhalo_ref
  32.1 0.0 copy-start
  32.1 1.0 %copy-done = f32[3,24,8,128]{3,2,1,0:T(8,128)S(1)} copy-done((f32[3,24,8,128]{3,2,1,0:T(8,128)S(1)}, f32[3,24,8,128]{3,2,1,0:T(8,128)}, u32[]{:S(2)}) %copy-start) | copy-done | bytes 294936
  33.1 0.0 copy-start.4
  33.1 1.9 %copy-done.4 = f32[1,1,128,48,128]{4,3,2,1,0:T(8,128)S(1)} copy-done((f32[1,1,128,48,128]{4,3,2,1,0:T(8,128)S(1)}, f32[1,1,128,48,128]{4,3,2,1,0:T(8,128)}, u32[]{:S(2)}) %copy-start.4) | copy-done | bytes 3145752
  34.9 0.0 copy-start.6
  34.9 0.9 %copy-done.6 = f32[24,8,128]{2,1,0:T(8,128)S(1)} copy-done((f32[24,8,128]{2,1,0:T(8,128)S(1)}, f32[24,8,128]{2,1,0:T(8,128)}, u32[]{:S(2)}) %copy-start.6) | copy-done | bytes 98328
  35.8 0.0 copy-start.7
  35.8 0.7 copy-done.7
  36.5 0.0 copy-start.1
  36.5 0.0 copy-start.2
  36.5 0.0 copy-start.3
  36.5 16.7 %shard_map.140 = (f32[3,24,8,128]{3,2,1,0:T(8,128)S(1)}, f32[3,8,128]{2,1,0:T(8,128)S(1)}, f32[3,24,128]{2,1,0:T(8,128)S(1)}, f32[3,128]{1,0:T(4,128)S(1)}, f32[6144,128]{1,0:T(8,128)}) custom-call(s32[8,48]{1,0:T(8,128)S(1)} %bitcast.17, f32[3,24,8,128]{3,2,1,0:T(8,128)S(1)} %copy-done, f32[3,8,128]{2,1,0:T(8,128)S(1)} %collective-permute-done.xhalo_ref, ...), custom_call_target="tpu_custom_call" | custom-call | flops 10000000000 | bytes 10000000 | tf_op jit(solution)/shard_map/pallas_call | solution.py:305
  53.2 5.1 %collective-permute-start.4 = (f32[3,24,128]{2,1,0:T(8,128)S(1)}, f32[3,24,128]{2,1,0:T(8,128)S(1)}, u32[]{:S(2)}, u32[]{:S(2)}) collective-permute-start(f32[3,24,128]{2,1,0:T(8,128)S(1)} %get-tuple-element.20), channel_id=1, source_target_pairs={{0,1},{1,2},{2,3},{3,4},{4,5},{5,6},{6,7},{8,9},{9,10},{10,11},{11... | collective-permute-start | bytes 110600 | tf_op jit(solution)/shard_map/ppermute | solution.py:322
  58.3 17.8 %collective-permute-start.3 = (f32[3,8,128]{2,1,0:T(8,128)S(1)}, f32[3,8,128]{2,1,0:T(8,128)S(1)}, u32[]{:S(2)}, u32[]{:S(2)}) collective-permute-start(f32[3,8,128]{2,1,0:T(8,128)S(1)} %get-tuple-element.19), channel_id=1, source_target_pairs={{0,8},{8,16},{16,24},{1,9},{9,17},{17,25},{2,10},{10,18},{18,26},{... | collective-permute-start | bytes 36872 | tf_op jit(solution)/shard_map/ppermute | solution.py:321
  76.1 1.9 %collective-permute-start.5 = (f32[3,128]{1,0:T(4,128)S(1)}, f32[3,128]{1,0:T(4,128)S(1)}, u32[]{:S(2)}, u32[]{:S(2)}) collective-permute-start(f32[3,128]{1,0:T(4,128)S(1)} %get-tuple-element.21), channel_id=1, source_target_pairs={{0,9},{1,10},{2,11},{3,12},{4,13},{5,14},{6,15},{8,17},{9,18},{10,... | collective-permute-start | bytes 4616 | tf_op jit(solution)/shard_map/ppermute | solution.py:323
  78.1 3.9 %collective-permute-done.5.cface_ref = f32[3,128]{1,0:T(4,128)S(1)} collective-permute-done((f32[3,128]{1,0:T(4,128)S(1)}, f32[3,128]{1,0:T(4,128)S(1)}, u32[]{:S(2)}, u32[]{:S(2)}) %collective-permute-start.5) | collective-permute-done | bytes 1568 | tf_op jit(solution)/shard_map/ppermute | solution.py:323
  81.9 0.0 collective-permute-done.3.xface_ref
  81.9 0.0 collective-permute-done.4.yface_ref
  81.9 0.0 copy-done.1
  81.9 0.0 copy-done.2
  82.0 0.0 copy-done.3
  82.0 0.9 %shard_map.141 = (f32[3,24,8,128]{3,2,1,0:T(8,128)}, f32[3,24,8,128]{3,2,1,0:T(8,128)}) custom-call(f32[3,24,8,128]{3,2,1,0:T(8,128)S(1)} %copy-done, f32[3,24,8,128]{3,2,1,0:T(8,128)S(1)} %copy-done.1, f32[3,24,8,128]{3,2,1,0:T(8,128)S(1)} %copy-done.2, f32[24,8,128]{2,1,0:T(8,128)S(1)} %copy-done.3, f32[3,24,8,128]{3,2,1,0:T(8,128)S(1)} %get-tuple-element.18.force_ref, ...), custom_call_target="tpu_custom_call" | custom-call | tf_op jit(solution)/shard_map/pallas_call | solution.py:325
  (1 shorter events, 0.0 us)
Async XLA Ops:
  1.6 30.5 %collective-permute-start.1 = (f32[3,24,128]{2,1,0:T(8,128)S(1)}, f32[3,24,128]{2,1,0:T(8,128)S(1)}, u32[]{:S(2)}, u32[]{:S(2)}) collective-permute-start(f32[3,24,128]{2,1,0:T(8,128)S(1)} %bitcast.21), channel_id=1, source_target_pairs={{1,0},{2,1},{3,2},{4,3},{5,4},{6,5},{7,6},{9,8},{10,9},{11,10},{12... | collective-permute-start | bytes 110600 | tf_op jit(solution)/shard_map/ppermute | solution.py:286
  5.3 26.7 %collective-permute-start = (f32[3,8,128]{2,1,0:T(8,128)S(1)}, f32[3,8,128]{2,1,0:T(8,128)S(1)}, u32[]{:S(2)}, u32[]{:S(2)}) collective-permute-start(f32[3,8,128]{2,1,0:T(8,128)S(1)} %slice_bitcast_fusion), channel_id=1, source_target_pairs={{8,0},{16,8},{24,16},{9,1},{17,9},{25,17},{10,2},{18,10},{26,18},{... | collective-permute-start | bytes 36872 | tf_op jit(solution)/shard_map/ppermute | solution.py:285
  8.9 23.1 %collective-permute-start.2 = (f32[3,128]{1,0:T(4,128)S(1)}, f32[3,128]{1,0:T(4,128)S(1)}, u32[]{:S(2)}, u32[]{:S(2)}) collective-permute-start(f32[3,128]{1,0:T(4,128)S(1)} %bitcast.22), channel_id=1, source_target_pairs={{9,0},{10,1},{11,2},{12,3},{13,4},{14,5},{15,6},{17,8},{18,9},{19,... | collective-permute-start | bytes 4616 | tf_op jit(solution)/shard_map/ppermute | solution.py:287
  11.7 0.9 %copy-start.5 = (f32[256,128]{1,0:T(8,128)S(1)}, f32[256,128]{1,0:T(8,128)}, u32[]{:S(2)}) copy-start(f32[256,128]{1,0:T(8,128)} %modes_ref.1) | copy-start | bytes 393220
  12.6 0.7 copy-start.8
  13.3 0.7 copy-start.9
  13.9 0.7 copy-start.10
  32.1 1.0 %copy-start = (f32[3,24,8,128]{3,2,1,0:T(8,128)S(1)}, f32[3,24,8,128]{3,2,1,0:T(8,128)}, u32[]{:S(2)}) copy-start(f32[3,24,8,128]{3,2,1,0:T(8,128)} %disp_ref.3) | copy-start | bytes 884740
  33.1 1.9 %copy-start.4 = (f32[1,1,128,48,128]{4,3,2,1,0:T(8,128)S(1)}, f32[1,1,128,48,128]{4,3,2,1,0:T(8,128)}, u32[]{:S(2)}) copy-start(f32[1,1,128,48,128]{4,3,2,1,0:T(8,128)} %param.18) | copy-start | bytes 9437188
  34.9 0.9 %copy-start.6 = (f32[24,8,128]{2,1,0:T(8,128)S(1)}, f32[24,8,128]{2,1,0:T(8,128)}, u32[]{:S(2)}) copy-start(f32[24,8,128]{2,1,0:T(8,128)} %stiff_ref.1) | copy-start | bytes 294916
  35.8 0.7 copy-start.7
  36.5 45.4 %copy-start.1 = (f32[3,24,8,128]{3,2,1,0:T(8,128)S(1)}, f32[3,24,8,128]{3,2,1,0:T(8,128)}, u32[]{:S(2)}) copy-start(f32[3,24,8,128]{3,2,1,0:T(8,128)} %velocity_ref.1) | copy-start | bytes 884740
  36.5 45.4 %copy-start.2 = (f32[3,24,8,128]{3,2,1,0:T(8,128)S(1)}, f32[3,24,8,128]{3,2,1,0:T(8,128)}, u32[]{:S(2)}) copy-start(f32[3,24,8,128]{3,2,1,0:T(8,128)} %external_ref.1) | copy-start | bytes 884740
  36.5 45.4 %copy-start.3 = (f32[24,8,128]{2,1,0:T(8,128)S(1)}, f32[24,8,128]{2,1,0:T(8,128)}, u32[]{:S(2)}) copy-start(f32[24,8,128]{2,1,0:T(8,128)} %mass_ref.1) | copy-start | bytes 294916
  53.2 28.7 %collective-permute-start.4 = (f32[3,24,128]{2,1,0:T(8,128)S(1)}, f32[3,24,128]{2,1,0:T(8,128)S(1)}, u32[]{:S(2)}, u32[]{:S(2)}) collective-permute-start(f32[3,24,128]{2,1,0:T(8,128)S(1)} %get-tuple-element.20), channel_id=1, source_target_pairs={{0,1},{1,2},{2,3},{3,4},{4,5},{5,6},{6,7},{8,9},{9,10},{10,11},{11... | collective-permute-start | bytes 110600 | tf_op jit(solution)/shard_map/ppermute | solution.py:322
  58.3 23.6 %collective-permute-start.3 = (f32[3,8,128]{2,1,0:T(8,128)S(1)}, f32[3,8,128]{2,1,0:T(8,128)S(1)}, u32[]{:S(2)}, u32[]{:S(2)}) collective-permute-start(f32[3,8,128]{2,1,0:T(8,128)S(1)} %get-tuple-element.19), channel_id=1, source_target_pairs={{0,8},{8,16},{16,24},{1,9},{9,17},{17,25},{2,10},{10,18},{18,26},{... | collective-permute-start | bytes 36872 | tf_op jit(solution)/shard_map/ppermute | solution.py:321
  76.1 5.8 %collective-permute-start.5 = (f32[3,128]{1,0:T(4,128)S(1)}, f32[3,128]{1,0:T(4,128)S(1)}, u32[]{:S(2)}, u32[]{:S(2)}) collective-permute-start(f32[3,128]{1,0:T(4,128)S(1)} %get-tuple-element.21), channel_id=1, source_target_pairs={{0,9},{1,10},{2,11},{3,12},{4,13},{5,14},{6,15},{8,17},{9,18},{10,... | collective-permute-start | bytes 4616 | tf_op jit(solution)/shard_map/ppermute | solution.py:323
where the time goes:
time: 84.6 us; the launch traced here: 82.9 us
  Pallas kernels  35 us (41%)
  starting transfers between devices  32.6 us (39%)
  local copies, waits for them, and re-layouts  10.6 us (13%)
  waiting for transfers between devices  3.89 us (5%)
    ppermute x1, starting transfers between devices, on_device(): xface = lax.ppermute(xface, 'gx', back(along_x))  17.8 us
    pallas_call x1, Pallas kernels, on_device(): pl.pallas_call(matrices_kernel, out_shape=(shape(points, 4 * count, dtype...  17.4 us
    pallas_call x1, Pallas kernels, on_device(): pl.pallas_call(main_kernel, out_shape=(shape(3, rows, columns, layers), s...  16.7 us
    unnamed x24, local copies, waits for them, and re-layouts  8.2 us
    ppermute x1, starting transfers between devices, on_device(): yface = lax.ppermute(yface, 'gy', back(along_y))  5.1 us
    ppermute x1, waiting for transfers between devices, on_device(): cface = lax.ppermute(cface, ('gx', 'gy'), back(both))  3.87 us
    ppermute x1, starting transfers between devices, on_device(): yhalo = lax.ppermute(displacement[:, :, 0], 'gy', along_y)  3.01 us
    ppermute x1, starting transfers between devices, on_device(): xhalo = lax.ppermute(displacement[:, 0], 'gx', along_x)  2.85 us
  transfers between devices with their start and end apart: 6, of which 1 were waited for; matrix products, arithmetic and copies ran while one was open for 3% of the time, Pallas kernels for 21%

commit v1 on v0

v1 whole, which is shorter than its diff:
```python
import functools

import jax
import jax.numpy as jnp
from jax import lax
from jax.experimental import pallas as pl
from jax.experimental.pallas import tpu as pltpu
from jax.sharding import PartitionSpec as P

ITERS = 3
STEP = 0.25
HIGHEST = lax.Precision.HIGHEST
F32 = jnp.float32
BF16 = jnp.bfloat16
VMEM = pl.BlockSpec(memory_space=pltpu.VMEM)
HBM = pl.BlockSpec(memory_space=pltpu.HBM)
SMEM = pl.BlockSpec(memory_space=pltpu.SMEM)


def split(x):
    high = x.astype(BF16)
    return high, (x - high.astype(F32)).astype(BF16)


def dot(a, b):
    return jnp.dot(a, b, preferred_element_type=F32)


def exact(a, b):
    return jnp.dot(a, b, precision=HIGHEST, preferred_element_type=F32)


def transposed_product(a, b):
    terms = []
    for x in (a, b):
        one = x.astype(BF16).astype(F32)
        two = (x - one).astype(BF16).astype(F32)
        terms.append((one, two, x - one - two))
    (a1, a2, a3), (b1, b2, b3) = terms
    left = jnp.concatenate([a1, a1, a2, a2, a1, a3], axis=0).astype(BF16)
    right = jnp.concatenate([b1, b2, b1, b2, b3, b1], axis=0).astype(BF16)
    return lax.dot_general(left, right, (((0,), (0,)), ((), ())), preferred_element_type=F32)


def inverse(matrix):
    size = matrix.shape[0]
    tile = (8, size)
    count = size // 8
    blocks = [matrix[i : i + 8] for i in range(0, size, 8)]
    lane = lax.broadcasted_iota(jnp.int32, tile, 1)
    row = lax.broadcasted_iota(jnp.int32, tile, 0)
    for b in range(count):
        before = panel = blocks[b]
        for s in range(0, 8, 2):
            k = b * 8 + s
            c0 = jnp.broadcast_to(panel[:, k : k + 1], tile)
            c1 = jnp.broadcast_to(panel[:, k + 1 : k + 2], tile)
            r0 = jnp.broadcast_to(panel[s : s + 1, :], tile)
            r1 = jnp.broadcast_to(panel[s + 1 : s + 2, :], tile)
            p00 = jnp.broadcast_to(c0[s : s + 1, :], tile)
            p10 = jnp.broadcast_to(c0[s + 1 : s + 2, :], tile)
            p11 = jnp.broadcast_to(c1[s + 1 : s + 2, :], tile)
            scale = 1.0 / (p00 * p11 - p10 * p10)
            q00, q10, q11 = p11 * scale, p10 * scale, p00 * scale
            r0, r1 = q00 * r0 - q10 * r1, q11 * r1 - q10 * r0
            n0 = jnp.where(lane == k, q00, jnp.where(lane == k + 1, -q10, r0))
            n1 = jnp.where(lane == k, -q10, jnp.where(lane == k + 1, q11, r1))
            both = jnp.logical_or(lane == k, lane == k + 1)
            rest = jnp.where(both, 0.0, panel) - c0 * n0 - c1 * n1
            panel = jnp.where(row == s, n0, jnp.where(row == s + 1, n1, rest))
        inside = jnp.logical_and(lane >= b * 8, lane < b * 8 + 8)
        panel = jnp.where(inside, -panel, panel)
        change = transposed_product(before, panel)
        for i in range(count):
            old = blocks[i]
            kept = jnp.where(inside, 0.0, old)
            if i == b:
                blocks[i] = panel
            elif i == b + 1:
                for s in range(8):
                    k = b * 8 + s
                    column = jnp.broadcast_to(old[:, k : k + 1], tile)
                    kept = kept - column * jnp.broadcast_to(panel[s : s + 1, :], tile)
                blocks[i] = kept
            else:
                blocks[i] = kept - change[i * 8 : i * 8 + 8]
    return -jnp.concatenate(blocks, axis=0)


def near(a, b):
    (ah, al), (bh, bl) = split(a), split(b)
    return dot(ah, bh) + dot(al, bh) + dot(ah, bl)


def fetch(sources, targets, sems):
    copies = [
        pltpu.make_async_copy(a, b, sems.at[i]) for i, (a, b) in enumerate(zip(sources, targets))
    ]
    for copy in copies:
        copy.start()
    for copy in copies:
        copy.wait()


def matrices_kernel(
    modes_hbm, local_hbm, weight_hbm, modulus_hbm, soft_hbm,
    start0_ref, start1_ref, high_ref, low_ref, back_ref, stress_ref,
    wide, modes_ref, local_ref, weight_ref, modulus_ref, soft_ref, sems,
):
    fetch(
        (modes_hbm, local_hbm, weight_hbm, modulus_hbm, soft_hbm),
        (modes_ref, local_ref, weight_ref, modulus_ref, soft_ref),
        sems,
    )
    points, count = modes_ref.shape
    modes = modes_ref[...]
    modes_t = modes.T
    weight = weight_ref[...] / points
    modulus = modulus_ref[...]
    root = jnp.sqrt(soft_ref[...])
    scale = weight * modulus / root
    inverted = inverse(exact(modes_t * (weight * modulus), modes))
    wide[...] = jnp.zeros_like(wide)
    wide[0 : local_ref.shape[0], :] = local_ref[...]
    local = wide[...]
    stress_ref[...] = (local * scale).astype(BF16)
    high, low = split(modes_t * root)
    start0_ref[0:count] = high
    start0_ref[count:] = high
    start1_ref[0:count] = low
    soft_local = local[0:8] * root
    local_high = soft_local.astype(BF16).astype(F32)
    part = [local_high, local_high, soft_local - local_high, jnp.zeros_like(local_high)]
    start1_ref[count:] = jnp.concatenate(part * (count // 32), axis=0).astype(BF16)
    back = near((modes_t * scale).T, inverted)
    high, low = split(back)
    back_ref[:, 0:count] = high
    back_ref[:, count:] = low
    newton = near(back, modes_t * root)
    high, low = split(newton)
    high_ref[...] = high
    low_ref[...] = low


def respond(u):
    return u * lax.rsqrt(1.0 + u * u)


def cells(states, strains, start0, start1, newton_high, newton_low, back, stress_m):
    layers = states[0].shape[1]
    count = states[0].shape[0]
    number = len(states)
    part = min(2, number)
    turned = [state.T for state in states]
    place = lax.broadcasted_iota(jnp.int32, (layers, count), 1) // 32
    strain_parts = []
    each = count // 32
    for q in range(0, number, each):
        rows = []
        for strain in strains[q : q + each]:
            high = strain.astype(BF16).astype(F32)
            rows += [high, strain - high, high, jnp.zeros_like(high)]
        rows = jnp.concatenate(rows, axis=0).T
        strain_parts += [jnp.where(place == g, rows, 0.0).astype(BF16) for g in range(each)]
    start = []
    for c in range(0, number, part):
        high, low = split(jnp.concatenate(turned[c : c + part], axis=0))
        strain = jnp.concatenate(strain_parts[c : c + part], axis=0)
        start.append(
            dot(jnp.concatenate([high, low], axis=1), start0)
            + dot(jnp.concatenate([high, strain], axis=1), start1)
        )
    now = start
    for step in range(ITERS - 1):
        later = []
        for u in now:
            high, low = split(respond(u))
            later.append(u - (dot(high, newton_high) + dot(low, newton_high) + dot(high, newton_low)))
        now = later
    last, moved = [], []
    for first, u in zip(start, now):
        h = respond(u)
        last.append(u - dot(h.astype(BF16), newton_high))
        moved.append(split(first - u + h))
    new_states, stresses = [], []
    for c, (high, low) in enumerate(moved):
        both = dot(high, back)
        change = both[:, 0:count] + both[:, count:] + dot(low, back[:, 0:count])
        for g in range(part):
            new_states.append(states[c * part + g] - change[g * layers : (g + 1) * layers].T)
    for u in last:
        stress = lax.dot_general(
            stress_m, respond(u).astype(BF16), (((1,), (1,)), ((), ())), preferred_element_type=F32
        )
        stresses += [stress[0:8, g * layers : (g + 1) * layers] for g in range(part)]
    return new_states, stresses


def pencil_rows(ref, q, g):
    groups, count, group, layers = ref.shape
    place = pl.ds(q * (count * group) + g, count, stride=group)
    return ref.reshape(groups * count * group, layers), place


def get_pencil(ref, q, g):
    flat, place = pencil_rows(ref, q, g)
    return flat[place, :]


def set_pencil(ref, q, g, value):
    flat, place = pencil_rows(ref, q, g)
    flat[place, :] = value


def edges_kernel(disp_hbm, xface_ref, yface_ref, corner_ref, disp_ref, sems):
    fetch((disp_hbm,), (disp_ref,), sems)
    for c in range(3):
        xface_ref[c] = disp_ref[c, 0]
        yface_ref[c] = disp_ref[c, :, 0, :]
        corner_ref[c : c + 1] = disp_ref[c, 0, 0:1]


def main_kernel(
    lists_ref, disp_ref, xhalo_ref, yhalo_ref, corner_ref, stiff_ref, state_hbm,
    start0_ref, start1_ref, high_ref, low_ref, back_ref, stress_ref,
    force_ref, xface_ref, yface_ref, cface_ref, out_hbm,
    strain_s, stress_s, state_s, out_s, in_sems, out_sems,
):
    rows, columns, layers = stiff_ref.shape
    groups, count, group, _ = state_s.shape
    pencils = rows * columns

    def load(q):
        return pltpu.make_async_copy(
            state_hbm.at[:, pl.ds(q * group, group), :], state_s.at[q], in_sems.at[q]
        )

    def store(q):
        return pltpu.make_async_copy(
            out_s.at[q], out_hbm.at[:, pl.ds(q * group, group), :], out_sems.at[q]
        )

    for q in range(groups):
        load(q).start()
    tile = (columns, layers)
    lane = lax.broadcasted_iota(jnp.int32, tile, 1)
    sub = lax.broadcasted_iota(jnp.int32, tile, 0)
    last_lane = lane == layers - 1
    first_lane = lane == 0
    last_sub = sub == columns - 1
    first_sub = sub == 0
    member = lax.axis_index("gy")

    def node_row(c, i):
        own = disp_ref[c, i] if i < rows else xhalo_ref[c]
        edge = yhalo_ref[c, i : i + 1] if i < rows else corner_ref[c : c + 1]
        up = jnp.where(last_sub, jnp.broadcast_to(edge, tile), pltpu.roll(own, columns - 1, 0))
        mean, diff = 0.5 * (up + own), up - own
        mean_up = jnp.where(last_lane, 0.0, pltpu.roll(mean, layers - 1, 1))
        diff_up = jnp.where(last_lane, 0.0, pltpu.roll(diff, layers - 1, 1))
        return 0.5 * (mean_up + mean), 0.5 * (diff_up + diff), mean_up - mean

    lower = [node_row(c, 0) for c in range(3)]
    zero_tile = jnp.zeros(tile, F32)
    for i in range(rows):
        upper = [node_row(c, i + 1) for c in range(3)]
        g = [
            (upper[c][0] - lower[c][0], 0.5 * (upper[c][1] + lower[c][1]), 0.5 * (upper[c][2] + lower[c][2]))
            for c in range(3)
        ]
        lower = upper
        strain = [g[0][0], g[1][1], g[2][2], g[1][2] + g[2][1], g[0][2] + g[2][0], g[0][1] + g[1][0]]
        stiffness = stiff_ref[i]
        volume = strain[0] + strain[1] + strain[2]
        for c in range(8):
            place = pl.ds(i * columns * 8 + c, columns, stride=8)
            if c >= 6:
                strain_s[place, :] = zero_tile
                continue
            strain_s[place, :] = strain[c]
            stress_s[place, :] = stiffness * (volume + 2.0 * strain[c] if c < 3 else strain[c])

    def body(q, carry):
        base = q * group
        load(q).wait()
        busy = lists_ref[member, base] >= 0

        @pl.when(busy)
        def _():
            entries = [lists_ref[member, base + g] for g in range(group)]
            states = [get_pencil(state_s, q, g) for g in range(group)]
            strains = [
                strain_s[pl.ds(pl.multiple_of(jnp.maximum(e, 0) * 8, 8), 8), :] for e in entries
            ]
            new_states, stresses = cells(
                states, strains, start0_ref[...], start1_ref[...], high_ref[...], low_ref[...],
                back_ref[...], stress_ref[...],
            )
            for g in range(group):
                set_pencil(out_s, q, g, jnp.where(entries[g] >= 0, new_states[g], 0.0))
                spot = jnp.where(entries[g] >= 0, entries[g], pencils)
                stress_s[pl.ds(pl.multiple_of(spot * 8, 8), 8), :] = stresses[g]

        @pl.when(jnp.logical_not(busy))
        def _():
            out_s[q] = jnp.zeros((count, group, layers), F32)

        store(q).start()
        return carry

    lax.fori_loop(0, groups, body, 0)

    def fluxes(s, side_mean, side_diff, lane_zero):
        def along(v):
            down = jnp.where(lane_zero, 0.0, pltpu.roll(v, 1, 1))
            return 0.5 * (v + down), v - down

        first = [along(side_mean(s[c]))[0] for c in (0, 5, 4)]
        second = [along(side_diff(s[c]))[0] for c in (5, 1, 3)]
        third = [along(side_mean(s[c]))[1] for c in (4, 3, 2)]
        half = [0.5 * (second[c] + third[c]) for c in range(3)]
        return [(first[c] + half[c], half[c] - first[c]) for c in range(3)]

    def shift(v):
        return jnp.where(first_sub, 0.0, pltpu.roll(v, 1, 0))

    below = None
    for i in range(rows):
        s = [stress_s[pl.ds(i * columns * 8 + c, columns, stride=8), :] for c in range(6)]
        here = fluxes(s, lambda v: 0.5 * (v + shift(v)), lambda v: v - shift(v), first_lane)
        for c in range(3):
            force_ref[c, i] = -here[c][0] if below is None else -(here[c][0] + below[c][1])
        below = here
    for c in range(3):
        xface_ref[c] = -below[c][1]
    s = [stress_s[pl.ds((columns - 1) * 8 + c, rows, stride=columns * 8), :] for c in range(6)]
    wide_zero = lax.broadcasted_iota(jnp.int32, (rows, layers), 1) == 0
    side = fluxes(s, lambda v: 0.5 * v, lambda v: -v, wide_zero)
    for c in range(3):
        yface_ref[c] = -side[c][0]
        yface_ref[c, 1:rows] = yface_ref[c, 1:rows] - side[c][1][0 : rows - 1]
        cface_ref[c : c + 1] = -side[c][1][rows - 1 : rows]
    for q in range(groups):
        store(q).wait()


def update_kernel(
    disp_ref, velocity_ref, external_ref, mass_ref, force_ref, xface_ref, yface_ref, cface_ref,
    disp_out, velocity_out,
):
    rows, columns, layers = mass_ref.shape
    first_sub = lax.broadcasted_iota(jnp.int32, (columns, layers), 0) == 0
    for i in range(rows):
        factor = STEP / mass_ref[i]
        for c in range(3):
            edge = yface_ref[c, i : i + 1]
            if i == 0:
                edge = edge + cface_ref[c : c + 1]
            internal = force_ref[c, i] + jnp.where(
                first_sub, jnp.broadcast_to(edge, (columns, layers)), 0.0
            )
            if i == 0:
                internal = internal + xface_ref[c]
            velocity = velocity_ref[c, i] + factor * (external_ref[c, i] - internal)
            velocity_out[c, i] = velocity
            disp_out[c, i] = disp_ref[c, i] + STEP * velocity


def shape(*dims, dtype=F32):
    return jax.ShapeDtypeStruct(dims, dtype)


def on_device(
    displacement, velocity, external_force, node_mass, stiffness, cloak_list, micro_state,
    localization, modes, point_weight, point_modulus, softening,
):
    rows, columns, layers = stiffness.shape
    points, count = modes.shape
    most = cloak_list.shape[2]
    gx, gy = lax.axis_size("gx"), lax.axis_size("gy")
    along_x = [(i + 1, i) for i in range(gx - 1)]
    along_y = [(i + 1, i) for i in range(gy - 1)]
    both = [((i + 1) * gy + j + 1, i * gy + j) for i in range(gx - 1) for j in range(gy - 1)]
    back = lambda pairs: [(b, a) for a, b in pairs]
    group = 8
    xhalo, yhalo, corner = pl.pallas_call(
        edges_kernel,
        out_shape=(shape(3, columns, layers), shape(3, rows, layers), shape(3, layers)),
        in_specs=[HBM],
        out_specs=(VMEM,) * 3,
        scratch_shapes=[pltpu.VMEM(displacement.shape, F32), pltpu.SemaphoreType.DMA((1,))],
        compiler_params=pltpu.CompilerParams(vmem_limit_bytes=4 * 2**20),
    )(displacement)
    xhalo = lax.ppermute(xhalo, "gx", along_x)
    yhalo = lax.ppermute(yhalo, "gy", along_y)
    corner = lax.ppermute(corner, ("gx", "gy"), both)

    matrices = pl.pallas_call(
        matrices_kernel,
        out_shape=tuple(shape(n, points, dtype=BF16) for n in (2 * count, 2 * count, points, points))
        + (shape(points, 2 * count, dtype=BF16), shape(16, points, dtype=BF16)),
        in_specs=[HBM] * 5,
        out_specs=(VMEM,) * 6,
        scratch_shapes=[
            pltpu.VMEM((16, points), F32), pltpu.VMEM((points, count), F32),
            pltpu.VMEM((localization.shape[1], points), F32),
        ]
        + [pltpu.VMEM((1, points), F32)] * 3
        + [pltpu.SemaphoreType.DMA((5,))],
        compiler_params=pltpu.CompilerParams(vmem_limit_bytes=16 * 2**20),
        cost_estimate=pl.CostEstimate(flops=10**10, bytes_accessed=10**6, transcendentals=0),
    )(
        modes, localization.T, point_weight.reshape(1, points), point_modulus.reshape(1, points),
        softening.reshape(1, points),
    )

    groups = most // group
    force, xface, yface, cface, new_state = pl.pallas_call(
        main_kernel,
        out_shape=(
            shape(3, rows, columns, layers), shape(3, columns, layers), shape(3, rows, layers),
            shape(3, layers), shape(count, most, layers),
        ),
        in_specs=[SMEM] + [VMEM] * 5 + [HBM] + [VMEM] * 6,
        out_specs=(VMEM,) * 4 + (HBM,),
        scratch_shapes=[
            pltpu.VMEM((rows * columns * 8, layers), F32),
            pltpu.VMEM((rows * columns * 8 + 8, layers), F32),
            pltpu.VMEM((groups, count, group, layers), F32),
            pltpu.VMEM((groups, count, group, layers), F32),
            pltpu.SemaphoreType.DMA((groups,)),
            pltpu.SemaphoreType.DMA((groups,)),
        ],
        compiler_params=pltpu.CompilerParams(vmem_limit_bytes=40 * 2**20),
        cost_estimate=pl.CostEstimate(flops=10**10, bytes_accessed=10**7, transcendentals=0),
    )(
        cloak_list[0], displacement, xhalo, yhalo, corner, stiffness,
        micro_state.reshape(count, most, layers), *matrices,
    )

    xface = lax.ppermute(xface, "gx", back(along_x))
    yface = lax.ppermute(yface, "gy", back(along_y))
    cface = lax.ppermute(cface, ("gx", "gy"), back(both))

    displacement_next, velocity_next = pl.pallas_call(
        update_kernel,
        out_shape=(shape(3, rows, columns, layers),) * 2,
        in_specs=[VMEM] * 8,
        out_specs=(VMEM,) * 2,
        compiler_params=pltpu.CompilerParams(vmem_limit_bytes=16 * 2**20),
    )(displacement, velocity, external_force, node_mass, force, xface, yface, cface)
    return displacement_next, velocity_next, new_state.reshape(micro_state.shape)


def solution(mesh):
    field = P(None, "gx", "gy", None)
    grid = P("gx", "gy", None)
    state = P("gx", "gy", None, None, None)
    in_specs = (field, field, field, grid, grid, P("gx", None, None), state, P(), P(), P(), P(), P())
    return jax.shard_map(
        on_device, mesh=mesh, in_specs=in_specs, out_specs=(field, field, state), check_vma=False
    )
```

time: 84.6 us -> 51.1 us (0.60); the launches traced: 82.9 us -> 51.1 us
  Pallas kernels: 35 us -> 19.1 us
  starting transfers between devices: 32.6 us -> 22.7 us
  local copies, waits for them, and re-layouts: 10.6 us -> 4.62 us
    pallas_call x1 -> x2, Pallas kernels: 17.4 us -> 9.21 us  [the longest x1 9.12 us: on_device(): pl.pallas_call(matrices_kernel, out_shape=tuple((shape(n, points, dtype=B...]
    ppermute x1, starting transfers between devices: 17.8 us -> 9.97 us  [on_device(): xface = lax.ppermute(xface, 'gx', back(along_x))]
    pallas_call x1, Pallas kernels: 16.7 us -> 8.92 us  [on_device(): pl.pallas_call(main_kernel, out_shape=(shape(3, rows, columns, layers), s...]
    unnamed x24 -> x26, local copies, waits for them, and re-layouts: 8.2 us -> 4.62 us
    ppermute x1, starting transfers between devices: 5.1 us -> 3.12 us  [on_device(): yface = lax.ppermute(yface, 'gy', back(along_y))]
    slice x2 -> x0, local copies, waits for them, and re-layouts: 1.69 us -> none  [the longest x1 0.98 us: on_device(): yhalo = lax.ppermute(displacement[:, :, 0], 'gy', along_y)]
  transfers between devices with their start and end apart: 6 -> 6, of which waited for: 1 -> 1; matrix products, arithmetic and copies ran while one was open for 3% -> 0% of each run, Pallas kernels for 21% -> 18%
where the time goes in v1:
time: 51.1 us
  starting transfers between devices  22.7 us (44%)
  Pallas kernels  19.1 us (37%)
  local copies, waits for them, and re-layouts  4.62 us (9%)
  waiting for transfers between devices  3.89 us (8%)
  between operations  0.83 us (2%)
    ppermute x1, starting transfers between devices, on_device(): xface = lax.ppermute(xface, 'gx', back(along_x))  9.97 us
    pallas_call x1, Pallas kernels, on_device(): pl.pallas_call(matrices_kernel, out_shape=tuple((shape(n, points, dtype=B...  9.12 us
    pallas_call x1, Pallas kernels, on_device(): pl.pallas_call(main_kernel, out_shape=(shape(3, rows, columns, layers), s...  8.92 us
    unnamed x26, local copies, waits for them, and re-layouts  4.62 us
    ppermute x1, waiting for transfers between devices, on_device(): cface = lax.ppermute(cface, ('gx', 'gy'), back(both))  3.87 us
    ppermute x1, starting transfers between devices, on_device(): corner = lax.ppermute(corner, ('gx', 'gy'), both)  3.57 us
    ppermute x1, starting transfers between devices, on_device(): yface = lax.ppermute(yface, 'gy', back(along_y))  3.12 us
    ppermute x1, starting transfers between devices, on_device(): yhalo = lax.ppermute(yhalo, 'gy', along_y)  2.16 us
  transfers between devices with their start and end apart: 6, of which 1 were waited for; matrix products, arithmetic and copies ran while one was open for 0% of the time, Pallas kernels for 18%

profile of v1, /device:TPU:25, one launch (start us, length us, event | category | flops | bytes accessed | tf_op | source)
XLA Modules:
  0.0 51.1 jit_solution(9108893083820089006)
XLA Ops:
  0.6 0.0 copy-start
  0.6 1.0 %copy-done = f32[3,24,8,128]{3,2,1,0:T(8,128)S(1)} copy-done((f32[3,24,8,128]{3,2,1,0:T(8,128)S(1)}, f32[3,24,8,128]{3,2,1,0:T(8,128)}, u32[]{:S(2)}) %copy-start) | copy-done | bytes 294936
  1.6 0.1 shard_map.139
  1.7 3.6 %collective-permute-start.2 = (f32[3,128]{1,0:T(4,128)S(1)}, f32[3,128]{1,0:T(4,128)S(1)}, u32[]{:S(2)}, u32[]{:S(2)}) collective-permute-start(f32[3,128]{1,0:T(4,128)S(1)} %get-tuple-element.21), channel_id=1, source_target_pairs={{9,0},{10,1},{11,2},{12,3},{13,4},{14,5},{15,6},{17,8},{18,9},{19,... | collective-permute-start | bytes 4616 | tf_op jit(solution)/shard_map/ppermute | solution.py:396
  5.3 1.9 %collective-permute-start = (f32[3,8,128]{2,1,0:T(8,128)S(1)}, f32[3,8,128]{2,1,0:T(8,128)S(1)}, u32[]{:S(2)}, u32[]{:S(2)}) collective-permute-start(f32[3,8,128]{2,1,0:T(8,128)S(1)} %get-tuple-element.19), channel_id=1, source_target_pairs={{8,0},{16,8},{24,16},{9,1},{17,9},{25,17},{10,2},{18,10},{26,18},{... | collective-permute-start | bytes 36872 | tf_op jit(solution)/shard_map/ppermute | solution.py:394
  7.2 2.2 %collective-permute-start.1 = (f32[3,24,128]{2,1,0:T(8,128)S(1)}, f32[3,24,128]{2,1,0:T(8,128)S(1)}, u32[]{:S(2)}, u32[]{:S(2)}) collective-permute-start(f32[3,24,128]{2,1,0:T(8,128)S(1)} %get-tuple-element.20), channel_id=1, source_target_pairs={{1,0},{2,1},{3,2},{4,3},{5,4},{6,5},{7,6},{9,8},{10,9},{11,10},{12... | collective-permute-start | bytes 110600 | tf_op jit(solution)/shard_map/ppermute | solution.py:395
  9.4 0.0 copy-start.6
  9.4 0.9 %copy-done.6 = f32[256,128]{1,0:T(8,128)S(1)} copy-done((f32[256,128]{1,0:T(8,128)S(1)}, f32[256,128]{1,0:T(8,128)}, u32[]{:S(2)}) %copy-start.6) | copy-done | bytes 131096
  10.3 0.0 copy-start.8
  10.3 0.7 %copy-done.8 = f32[256,6]{0,1:T(8,128)S(1)} copy-done((f32[256,6]{0,1:T(8,128)S(1)}, f32[256,6]{0,1:T(8,128)}, u32[]{:S(2)}) %copy-start.8) | copy-done | bytes 6168
  11.0 0.0 copy-start.10
  11.0 0.7 %copy-done.10 = f32[256]{0:T(256)S(1)} copy-done((f32[256]{0:T(256)S(1)}, f32[256]{0:T(256)}, u32[]{:S(2)}) %copy-start.10) | copy-done | bytes 1048
  11.6 0.0 copy-start.11
  11.7 0.7 %copy-done.11 = f32[256]{0:T(256)S(1)} copy-done((f32[256]{0:T(256)S(1)}, f32[256]{0:T(256)}, u32[]{:S(2)}) %copy-start.11) | copy-done | bytes 1048
  12.3 0.0 copy-start.12
  12.3 0.7 %copy-done.12 = f32[256]{0:T(256)S(1)} copy-done((f32[256]{0:T(256)S(1)}, f32[256]{0:T(256)}, u32[]{:S(2)}) %copy-start.12) | copy-done | bytes 1048
  13.0 0.0 copy-start.1
  13.0 0.0 copy-start.5
  13.0 0.0 copy-start.7
  13.0 0.0 copy-start.9
  13.0 9.1 %shard_map.140 = (bf16[256,256]{1,0:T(8,128)(2,1)S(1)}, bf16[256,256]{1,0:T(8,128)(2,1)S(1)}, bf16[256,256]{1,0:T(8,128)(2,1)S(1)}, bf16[256,256]{1,0:T(8,128)(2...) custom-call(f32[256,128]{1,0:T(8,128)S(1)} %copy-done.6, f32[6,256]{1,0:T(8,128)S(1)} %bitcast.8, ...), custom_call_target="tpu_custom_call" | custom-call | flops 10000000000 | bytes 1000000 | tf_op jit(solution)/shard_map/pallas_call | solution.py:398
  22.1 0.0 collective-permute-done.2.corner_ref
  22.2 0.0 collective-permute-done.xhalo_ref
  22.2 0.0 collective-permute-done.1.yhalo_ref
  22.2 0.0 copy-done.1
  22.2 0.0 copy-done.5
  22.2 0.0 copy-done.7
  22.2 0.0 copy-done.9
  22.2 0.0 copy-start.2
  22.2 0.0 copy-start.3
  22.2 0.0 copy-start.4
  22.3 8.9 %shard_map.141 = (f32[3,24,8,128]{3,2,1,0:T(8,128)S(1)}, f32[3,8,128]{2,1,0:T(8,128)S(1)}, f32[3,24,128]{2,1,0:T(8,128)S(1)}, f32[3,128]{1,0:T(4,128)S(1)}, f32[128,48,128]{2,1,0:T(8,128)}) custom-call(s32[8,48]{1,0:T(8,128)S(1)} %bitcast.9, f32[3,24,8,128]{3,2,1,0:T(8,128)S(1)} %copy-done.1, f32[3,8,128]{2,1,0:T(8,128)S(1)} %collective-permute-done.xhalo_ref, ...), custom_call_target="tpu_custom_call" | custom-call | flops 10000000000 | bytes 10000000 | tf_op jit(solution)/shard_map/pallas_call | solution.py:418
  31.2 3.1 %collective-permute-start.4 = (f32[3,24,128]{2,1,0:T(8,128)S(1)}, f32[3,24,128]{2,1,0:T(8,128)S(1)}, u32[]{:S(2)}, u32[]{:S(2)}) collective-permute-start(f32[3,24,128]{2,1,0:T(8,128)S(1)} %get-tuple-element.30), channel_id=1, source_target_pairs={{0,1},{1,2},{2,3},{3,4},{4,5},{5,6},{6,7},{8,9},{9,10},{10,11},{11... | collective-permute-start | bytes 110600 | tf_op jit(solution)/shard_map/ppermute | solution.py:442
  34.3 10.0 %collective-permute-start.3 = (f32[3,8,128]{2,1,0:T(8,128)S(1)}, f32[3,8,128]{2,1,0:T(8,128)S(1)}, u32[]{:S(2)}, u32[]{:S(2)}) collective-permute-start(f32[3,8,128]{2,1,0:T(8,128)S(1)} %get-tuple-element.29), channel_id=1, source_target_pairs={{0,8},{8,16},{16,24},{1,9},{9,17},{17,25},{2,10},{10,18},{18,26},{... | collective-permute-start | bytes 36872 | tf_op jit(solution)/shard_map/ppermute | solution.py:441
  44.3 1.9 %collective-permute-start.5 = (f32[3,128]{1,0:T(4,128)S(1)}, f32[3,128]{1,0:T(4,128)S(1)}, u32[]{:S(2)}, u32[]{:S(2)}) collective-permute-start(f32[3,128]{1,0:T(4,128)S(1)} %get-tuple-element.31), channel_id=1, source_target_pairs={{0,9},{1,10},{2,11},{3,12},{4,13},{5,14},{6,15},{8,17},{9,18},{10,... | collective-permute-start | bytes 4616 | tf_op jit(solution)/shard_map/ppermute | solution.py:443
  46.2 3.9 %collective-permute-done.5.cface_ref = f32[3,128]{1,0:T(4,128)S(1)} collective-permute-done((f32[3,128]{1,0:T(4,128)S(1)}, f32[3,128]{1,0:T(4,128)S(1)}, u32[]{:S(2)}, u32[]{:S(2)}) %collective-permute-start.5) | collective-permute-done | bytes 1568 | tf_op jit(solution)/shard_map/ppermute | solution.py:443
  50.1 0.0 collective-permute-done.3.xface_ref
  50.1 0.0 collective-permute-done.4.yface_ref
  50.1 0.0 copy-done.2
  50.1 0.0 copy-done.3
  50.1 0.0 copy-done.4
  50.1 0.9 %shard_map.142 = (f32[3,24,8,128]{3,2,1,0:T(8,128)}, f32[3,24,8,128]{3,2,1,0:T(8,128)}) custom-call(f32[3,24,8,128]{3,2,1,0:T(8,128)S(1)} %copy-done.1, f32[3,24,8,128]{3,2,1,0:T(8,128)S(1)} %copy-done.2, f32[3,24,8,128]{3,2,1,0:T(8,128)S(1)} %copy-done.3, f32[24,8,128]{2,1,0:T(8,128)S(1)} %copy-done.4, f32[3,24,8,128]{3,2,1,0:T(8,128)S(1)} %get-tuple-element.28.force_ref, ...), custom_call_target="tpu_custom_call" | custom-call | tf_op jit(solution)/shard_map/pallas_call | solution.py:445
Async XLA Ops:
  0.6 1.0 %copy-start = (f32[3,24,8,128]{3,2,1,0:T(8,128)S(1)}, f32[3,24,8,128]{3,2,1,0:T(8,128)}, u32[]{:S(2)}) copy-start(f32[3,24,8,128]{3,2,1,0:T(8,128)} %disp_ref.3) | copy-start | bytes 884740
  1.7 20.5 %collective-permute-start.2 = (f32[3,128]{1,0:T(4,128)S(1)}, f32[3,128]{1,0:T(4,128)S(1)}, u32[]{:S(2)}, u32[]{:S(2)}) collective-permute-start(f32[3,128]{1,0:T(4,128)S(1)} %get-tuple-element.21), channel_id=1, source_target_pairs={{9,0},{10,1},{11,2},{12,3},{13,4},{14,5},{15,6},{17,8},{18,9},{19,... | collective-permute-start | bytes 4616 | tf_op jit(solution)/shard_map/ppermute | solution.py:396
  5.3 16.9 %collective-permute-start = (f32[3,8,128]{2,1,0:T(8,128)S(1)}, f32[3,8,128]{2,1,0:T(8,128)S(1)}, u32[]{:S(2)}, u32[]{:S(2)}) collective-permute-start(f32[3,8,128]{2,1,0:T(8,128)S(1)} %get-tuple-element.19), channel_id=1, source_target_pairs={{8,0},{16,8},{24,16},{9,1},{17,9},{25,17},{10,2},{18,10},{26,18},{... | collective-permute-start | bytes 36872 | tf_op jit(solution)/shard_map/ppermute | solution.py:394
  7.2 15.0 %collective-permute-start.1 = (f32[3,24,128]{2,1,0:T(8,128)S(1)}, f32[3,24,128]{2,1,0:T(8,128)S(1)}, u32[]{:S(2)}, u32[]{:S(2)}) collective-permute-start(f32[3,24,128]{2,1,0:T(8,128)S(1)} %get-tuple-element.20), channel_id=1, source_target_pairs={{1,0},{2,1},{3,2},{4,3},{5,4},{6,5},{7,6},{9,8},{10,9},{11,10},{12... | collective-permute-start | bytes 110600 | tf_op jit(solution)/shard_map/ppermute | solution.py:395
  9.4 0.9 %copy-start.6 = (f32[256,128]{1,0:T(8,128)S(1)}, f32[256,128]{1,0:T(8,128)}, u32[]{:S(2)}) copy-start(f32[256,128]{1,0:T(8,128)} %modes_hbm.1) | copy-start | bytes 393220
  10.3 0.7 %copy-start.8 = (f32[256,6]{0,1:T(8,128)S(1)}, f32[256,6]{0,1:T(8,128)}, u32[]{:S(2)}) copy-start(f32[256,6]{0,1:T(8,128)} %param.19) | copy-start | bytes 18436
  11.0 0.7 %copy-start.10 = (f32[256]{0:T(256)S(1)}, f32[256]{0:T(256)}, u32[]{:S(2)}) copy-start(f32[256]{0:T(256)} %param.21) | copy-start | bytes 3076
  11.6 0.7 %copy-start.11 = (f32[256]{0:T(256)S(1)}, f32[256]{0:T(256)}, u32[]{:S(2)}) copy-start(f32[256]{0:T(256)} %param.22) | copy-start | bytes 3076
  12.3 0.7 %copy-start.12 = (f32[256]{0:T(256)S(1)}, f32[256]{0:T(256)}, u32[]{:S(2)}) copy-start(f32[256]{0:T(256)} %param.23) | copy-start | bytes 3076
  13.0 9.2 %copy-start.1 = (f32[3,24,8,128]{3,2,1,0:T(8,128)S(1)}, f32[3,24,8,128]{3,2,1,0:T(8,128)}, u32[]{:S(2)}) copy-start(f32[3,24,8,128]{3,2,1,0:T(8,128)} %disp_ref.3) | copy-start | bytes 884740
  13.0 9.2 %copy-start.5 = (f32[1,1,128,48,128]{4,3,2,1,0:T(8,128)S(1)}, f32[1,1,128,48,128]{4,3,2,1,0:T(8,128)}, u32[]{:S(2)}) copy-start(f32[1,1,128,48,128]{4,3,2,1,0:T(8,128)} %param.18) | copy-start | bytes 9437188
  13.0 9.2 %copy-start.7 = (f32[24,8,128]{2,1,0:T(8,128)S(1)}, f32[24,8,128]{2,1,0:T(8,128)}, u32[]{:S(2)}) copy-start(f32[24,8,128]{2,1,0:T(8,128)} %stiff_ref.1) | copy-start | bytes 294916
  13.0 9.2 %copy-start.9 = (s32[1,8,48]{2,1,0:T(8,128)S(1)}, s32[1,8,48]{2,1,0:T(8,128)}, u32[]{:S(2)}) copy-start(s32[1,8,48]{2,1,0:T(8,128)} %param.17) | copy-start | bytes 4612
  22.2 27.9 %copy-start.2 = (f32[3,24,8,128]{3,2,1,0:T(8,128)S(1)}, f32[3,24,8,128]{3,2,1,0:T(8,128)}, u32[]{:S(2)}) copy-start(f32[3,24,8,128]{3,2,1,0:T(8,128)} %velocity_ref.1) | copy-start | bytes 884740
  22.2 27.9 %copy-start.3 = (f32[3,24,8,128]{3,2,1,0:T(8,128)S(1)}, f32[3,24,8,128]{3,2,1,0:T(8,128)}, u32[]{:S(2)}) copy-start(f32[3,24,8,128]{3,2,1,0:T(8,128)} %external_ref.1) | copy-start | bytes 884740
  22.2 27.9 %copy-start.4 = (f32[24,8,128]{2,1,0:T(8,128)S(1)}, f32[24,8,128]{2,1,0:T(8,128)}, u32[]{:S(2)}) copy-start(f32[24,8,128]{2,1,0:T(8,128)} %mass_ref.1) | copy-start | bytes 294916
  31.2 18.9 %collective-permute-start.4 = (f32[3,24,128]{2,1,0:T(8,128)S(1)}, f32[3,24,128]{2,1,0:T(8,128)S(1)}, u32[]{:S(2)}, u32[]{:S(2)}) collective-permute-start(f32[3,24,128]{2,1,0:T(8,128)S(1)} %get-tuple-element.30), channel_id=1, source_target_pairs={{0,1},{1,2},{2,3},{3,4},{4,5},{5,6},{6,7},{8,9},{9,10},{10,11},{11... | collective-permute-start | bytes 110600 | tf_op jit(solution)/shard_map/ppermute | solution.py:442
  34.3 15.8 %collective-permute-start.3 = (f32[3,8,128]{2,1,0:T(8,128)S(1)}, f32[3,8,128]{2,1,0:T(8,128)S(1)}, u32[]{:S(2)}, u32[]{:S(2)}) collective-permute-start(f32[3,8,128]{2,1,0:T(8,128)S(1)} %get-tuple-element.29), channel_id=1, source_target_pairs={{0,8},{8,16},{16,24},{1,9},{9,17},{17,25},{2,10},{10,18},{18,26},{... | collective-permute-start | bytes 36872 | tf_op jit(solution)/shard_map/ppermute | solution.py:441
  44.3 5.8 %collective-permute-start.5 = (f32[3,128]{1,0:T(4,128)S(1)}, f32[3,128]{1,0:T(4,128)S(1)}, u32[]{:S(2)}, u32[]{:S(2)}) collective-permute-start(f32[3,128]{1,0:T(4,128)S(1)} %get-tuple-element.31), channel_id=1, source_target_pairs={{0,9},{1,10},{2,11},{3,12},{4,13},{5,14},{6,15},{8,17},{9,18},{10,... | collective-permute-start | bytes 4616 | tf_op jit(solution)/shard_map/ppermute | solution.py:443
